TPU v7x, 128 devices: a whole 4x4x4 slice. The times are simulated.
128 devices in a mesh: gx: 16 (over z, y_lo, core), gy: 8 (over x, y_hi).
Axes of the slice: x: 4, y: 4 (y_hi: 2, y_lo: 2; y = y_hi * 2 + y_lo), z: 4, core: 2. Of those that a mesh axis runs over, the one named last changes fastest.
Arguments:
- phi: bfloat16 [2048, 80, 4, 256], P('gx', 'gy'), may hold values from -1 to 1, as said below
- potential: float32 [80, 4, 256], P('gy'), may hold values from 0 to 2
- kernel: bfloat16 [2048, 2048], P('gx'), may hold values from -0.25 to 0.25
- mask_s: int32 [32, 32], P('gx'), may hold values from 0 to 1, as said below
- mask_k: int32 [32, 32], P('gx'), may hold values from 0 to 1, as said below
Outputs:
- kernel_next: float32 [2048, 2048], P('gx', 'gy')
Inputs may be any that keep to these rules, and one draw needn't show every extreme that they name: `phi`: each block of 64 NGWFs has a box of 2 * max(13, 1) + 1 planes along the first grid dimension (periodic) around its centre; every NGWF is zero outside its block's box. mask_s[a, b] is 1 exactly where the periodic distance of the box centres of blocks a and b is at most h + h // 2, with h = max(13, 1); it is symmetric with ones on the diagonal. mask_k is symmetric, 1 wherever the centre distance is at most 3 h, and 1 for some further pairs.
All inputs are finite; a program needn't handle non-finite values.
Results may differ from a plain program's by a relative error of at most 0.0046.
Values may be sent and summed in bfloat16 or wider, within the bound.
No kernel may reach another device: no remote copies, remote signals or barrier semaphores. Data moves between devices by JAX's collectives and lax.ppermute only.
A program may use at most 192 MiB of HBM per device.

v0:
```python
import jax
import jax.numpy as jnp
from jax import lax
from jax.sharding import PartitionSpec as P

BLOCK = 64


def extended(block, sides, width):
    for axis, dim in sides:
        count = lax.axis_size(axis)
        forward = [(i, i + 1) for i in range(count - 1)]
        forward.append((count - 1, 0))
        backward = [(target, source) for source, target in forward]
        low = lax.ppermute(
            lax.slice_in_dim(block, block.shape[dim] - width, None, axis=dim), axis, forward
        )
        high = lax.ppermute(lax.slice_in_dim(block, 0, width, axis=dim), axis, backward)
        block = jnp.concatenate([low, block, high], axis=dim)
    return block


def spread(values, mask):
    rows, cols = (values.shape[-2], values.shape[-1])
    grid = values.reshape(values.shape[:-2] + (rows // BLOCK, BLOCK, cols // BLOCK, BLOCK))
    return (grid * mask.astype(values.dtype)[:, None, :, None]).reshape(values.shape)


def matmul(left, right):
    return jnp.dot(left, right, preferred_element_type=jnp.float32)


def shards(phi, potential, kernel, mask_s, mask_k):
    nrows = phi.shape[0]
    total = kernel.shape[1]
    width = total // lax.axis_size("gy")
    col_start = lax.axis_index("gy") * width
    padded = extended(phi, (("gy", 1),), 1).astype(jnp.float32)
    center = padded[:, 1:-1]
    lap = padded[:, 2:] + padded[:, :-2] - 6.0 * center
    for axis in (2, 3):
        lap = lap + jnp.roll(center, 1, axis) + jnp.roll(center, -1, axis)
    hphi = (-0.5 * lap + potential[None] * center).astype(jnp.bfloat16)
    flat_phi = phi.reshape(nrows, -1)
    flat_h = hphi.reshape(nrows, -1)
    piece = lax.all_gather(phi, "gx", axis=0, tiled=True)
    other = piece.reshape(piece.shape[0], -1)
    s_part = jnp.einsum("ap,bp->ab", flat_phi, other, preferred_element_type=jnp.float32)
    h_part = jnp.einsum("ap,bp->ab", flat_h, other, preferred_element_type=jnp.float32)
    partial_sums = jnp.stack([s_part, h_part])
    mask_cols = lax.dynamic_slice_in_dim(mask_s, col_start // BLOCK, width // BLOCK, 1)
    local = lax.psum_scatter(partial_sums, "gy", scatter_dimension=2, tiled=True)
    block_pair = spread(local, mask_cols).astype(jnp.bfloat16)
    rows = lax.all_gather(block_pair, "gy", axis=2, tiled=True)
    s_rows = rows[0]
    h_rows = rows[1]
    k_mat = spread(kernel, mask_k)
    pieces = lax.all_gather(block_pair, "gx", axis=1, tiled=True)
    x_acc = matmul(k_mat, pieces[0])
    y_acc = matmul(k_mat, pieces[1])
    pair = jnp.stack([x_acc.astype(jnp.bfloat16), y_acc.astype(jnp.bfloat16)])
    columns = lax.all_gather(pair, "gx", axis=1, tiled=True)
    p_one = matmul(h_rows, columns[0])
    p_two = matmul(s_rows, columns[1])
    z_mat = matmul(s_rows, columns[0])
    trio = jnp.stack([p_one, z_mat, p_two]).astype(jnp.bfloat16)
    trio_rows = lax.all_gather(trio, "gy", axis=2, tiled=True)
    q_mat = (
        matmul(trio_rows[0], columns[0])
        + matmul(trio_rows[1], columns[1])
        + matmul(trio_rows[2], columns[0])
    )
    grad = 3.0 * (trio[0].astype(jnp.float32) + trio[2].astype(jnp.float32)) - 2.0 * q_mat
    mask_kcols = lax.dynamic_slice_in_dim(mask_k, col_start // BLOCK, width // BLOCK, 1)
    kernel_cols = lax.dynamic_slice_in_dim(kernel, col_start, width, 1).astype(jnp.float32)
    return kernel_cols - 0.5 * spread(grad, mask_kcols)


def solution(mesh):
    in_specs = (
        P("gx", "gy", None, None),
        P("gy", None, None),
        P("gx", None),
        P("gx", None),
        P("gx", None),
    )
    out_specs = P("gx", "gy")
    return jax.shard_map(shards, mesh=mesh, in_specs=in_specs, out_specs=out_specs, check_vma=False)
```

profile of v0, /device:TPU:1, one launch (start us, length us, event | category | flops | bytes accessed | tf_op | source)
XLA Modules:
  0.0 531.0 jit_solution(17213908020200179331)
XLA Ops:
  6.5 4.1 copy.7
  10.6 0.0 all-gather.6.cloned.1.call-update
  10.6 0.0 reduce-scatter.2.cloned.1.call-start
  10.7 0.2 fusion.31
  10.9 3.8 collective-permute-start
  14.7 2.3 collective-permute-start.1
  17.0 10.3 %collective-permute-done = bf16[128,1,4,256]{3,2,1,0:T(4,128)(2,1)S(1)} collective-permute-done((bf16[128,1,4,256]{3,2,1,0:T(4,128)(2,1)S(1)}, bf16[128,1,4,256]{3,2,1,0:T(4,128)(2,1)S(1)}, u32[]{:S(2)}, u32[]{:S(2)}) %collective-permute-start) | collective-permute-done | bytes 262176 | tf_op jit(solution)/shard_map/ppermute | solution.py:15
  27.3 4.3 collective-permute-done.1
  31.6 2.1 maximum_convert_fusion
  33.7 4.4 fusion.29
  38.1 3.6 fusion.27
  41.7 11.8 %fusion.30 = (f32[128,10,4,255]{3,2,1,0:T(4,128)}, f32[128,10,4,255]{3,2,1,0:T(4,128)}) fusion(f32[128,12,4,256]{3,2,1,0:T(4,128)} %copy-done), kind=kLoop, calls=%fused_computation.53 | loop fusion | bytes 20889600 | tf_op jit(solution)/shard_map/jit(_roll_static)/slice | solution.py:42
  53.5 10.7 %fusion.28 = (f32[128,10,3,256]{3,2,1,0:T(4,128)}, f32[128,10,3,256]{3,2,1,0:T(4,128)}) fusion(f32[128,12,4,256]{3,2,1,0:T(4,128)} %copy-done), kind=kLoop, calls=%fused_computation.51 | loop fusion | bytes 15728640 | tf_op jit(solution)/shard_map/jit(_roll_static)/slice | solution.py:42
  64.2 19.3 %fusion.7 = bf16[128,10,4,256]{3,2,1,0:T(4,128)(2,1)} fusion(f32[128,10,4,1]{3,2,1,0:T(4,128)} %get-tuple-element.10, f32[128,10,4,255]{3,2,1,0:T(4,128)} %get-tuple-element.12, f32[128,10,4,255]{3,2,1,0:T(4,128)} %get-tuple-element.11, f32[128,10,4,1]{3,2,1,0:T(4,128)} %get-tuple-element.9, f32[128,10,1,256]{3,2,1,0:T(1,128)} %get-tuple-element.6, ...), kind=kLoop, calls=%fused_computation.8 | loop fusion | flops 19660800 | bytes 39362560 | tf_op jit(solution)/shard_map/convert_element_type | solution.py:43
  83.5 142.8 %all-gather.6.cloned.1.call-done = bf16[2048,10,4,256]{3,0,2,1:T(8,128)(2,1)} async-done(((bf16[128,10,4,256]{3,0,2,1:T(8,128)(2,1)}), bf16[2048,10,4,256]{3,0,2,1:T(8,128)(2,1)}) %all-gather.6.cloned.1.call-update) | async-done | bytes 41943056 | tf_op jit(solution)/shard_map/all_gather | solution.py:46
  226.3 18.8 %convolution_bitcast_fusion = f32[1,128,2048]{2,1,0:T(8,128)S(1)} fusion(bf16[2048,10,4,256]{3,0,2,1:T(8,128)(2,1)} %all-gather.6.cloned.1.call-done, bf16[128,10,4,256]{3,2,1,0:T(4,128)(2,1)S(1)} %copy-done.1), kind=kOutput, calls=%fused_computation.13 | convolution fusion | flops 5368709120 | bytes 45613056 | tf_op jit(solution)/shard_map/ap,bp->ab/dot_general | solution.py:48
  245.1 18.7 %fusion.10 = f32[1,128,2048]{2,1,0:T(8,128)S(1)} fusion(bf16[2048,10,4,256]{3,0,2,1:T(8,128)(2,1)} %all-gather.6.cloned.1.call-done, bf16[128,10,4,256]{3,2,1,0:T(4,128)(2,1)S(1)} %copy-done.2), kind=kOutput, calls=%fused_computation.12 | convolution fusion | flops 5368709120 | bytes 45613056 | tf_op jit(solution)/shard_map/ap,bp->ab/dot_general | solution.py:49
  263.8 1.5 pad_maximum_fusion
  265.4 0.0 all-gather.10.cloned.1.call-start
  265.5 0.1 dynamic-slice_convert_fusion
  265.5 0.1 mul.86
  265.6 0.2 mul.87
  265.9 75.5 %reduce-scatter.2.cloned.1.call-done = f32[2,128,256]{2,1,0:T(8,128)} async-done(((f32[2,128,2048]{2,1,0:T(8,128)}), f32[2,128,256]{2,1,0:T(8,128)}) %reduce-scatter.2.cloned.1.call-update) | async-done | bytes 262160 | tf_op jit(solution)/shard_map/reduce_scatter | solution.py:52
  341.4 1.6 multiply_convert_fusion
  343.0 0.0 all-gather.10.cloned.1.call-update
  343.0 0.0 all-gather.8.cloned.1.call-start
  343.1 0.5 all-gather.8.cloned.1.call-update
  343.6 0.0 all-gather.12.cloned.1.call-start
  343.7 0.2 mul.90
  343.9 0.8 mul.91
  344.7 33.4 %all-gather.10.cloned.1.call-done = bf16[2,2048,256]{2,1,0:T(8,128)(2,1)} async-done(((bf16[2,128,256]{2,1,0:T(8,128)(2,1)}), bf16[2,2048,256]{2,1,0:T(8,128)(2,1)}) %all-gather.10.cloned.1.call-update) | async-done | bytes 2097168 | tf_op jit(solution)/shard_map/all_gather | solution.py:58
  378.1 1.5 fusion.18
  379.6 1.5 fusion.19
  381.1 0.7 pad_maximum_fusion.2
  381.8 0.0 all-gather.14.cloned.1.call-start
  381.9 44.6 %all-gather.8.cloned.1.call-done = bf16[2,128,2048]{2,1,0:T(8,128)(2,1)} async-done(((bf16[2,128,256]{2,1,0:T(8,128)(2,1)}), bf16[2,128,2048]{2,1,0:T(8,128)(2,1)}) %all-gather.8.cloned.1.call-update) | async-done | bytes 1048592 | tf_op jit(solution)/shard_map/all_gather | solution.py:54
  426.5 36.4 %all-gather.12.cloned.1.call-done = bf16[2,2048,256]{2,1,0:T(8,128)(2,1)} async-done(((bf16[2,128,256]{2,1,0:T(8,128)(2,1)}), bf16[2,2048,256]{2,1,0:T(8,128)(2,1)}) %all-gather.12.cloned.1.call-update) | async-done | bytes 2097168 | tf_op jit(solution)/shard_map/all_gather | solution.py:62
  462.9 1.8 fusion.20
  464.8 1.7 fusion.22
  466.5 0.3 fusion.21
  466.8 0.7 pad_maximum_fusion.1
  467.5 0.0 all-gather.14.cloned.1.call-update
  467.5 0.1 mul.98
  467.6 0.2 mul.99
  467.8 50.6 %all-gather.14.cloned.1.call-done = bf16[3,128,2048]{2,1,0:T(8,128)(2,1)} async-done(((bf16[3,128,256]{2,1,0:T(8,128)(2,1)}), bf16[3,128,2048]{2,1,0:T(8,128)(2,1)}) %all-gather.14.cloned.1.call-update) | async-done | bytes 1572880 | tf_op jit(solution)/shard_map/all_gather | solution.py:67
  518.4 1.7 fusion.23
  520.1 1.7 convolution_add_fusion.1
  521.8 2.4 fusion.17
  (22 shorter events, 0.1 us)
Async XLA Ops:
  6.5 4.1 copy-start.1
  6.5 219.8 %all-gather.6.cloned.1.call-start = ((), (), s32[]{:S(2)}) async-start(), calls=%async_computation.1 | async-start | bytes 44564480 | tf_op jit(solution)/shard_map/all_gather | solution.py:46
  10.6 330.8 %reduce-scatter.2.cloned.1.call-start = ((), (), s32[]{:S(2)}) async-start(), calls=%async_computation.2 | async-start | bytes 2359296 | tf_op jit(solution)/shard_map/reduce_scatter | solution.py:52
  10.9 16.4 %collective-permute-start = (bf16[128,1,4,256]{3,2,1,0:T(4,128)(2,1)S(1)}, bf16[128,1,4,256]{3,2,1,0:T(4,128)(2,1)S(1)}, u32[]{:S(2)}, u32[]{:S(2)}) collective-permute-start(bf16[128,1,4,256]{3,2,1,0:T(4,128)(2,1)S(1)} %get-tuple-element.13), channel_id=1, source_target_pairs={{0,1},{1,2},{2,3},{3,4},{4,5},{5,6},{6,7},{7,0},{8,9},{9,10},{10,1... | collective-permute-start | bytes 786440 | tf_op jit(solution)/shard_map/ppermute | solution.py:15
  14.7 16.9 %collective-permute-start.1 = (bf16[128,1,4,256]{3,2,1,0:T(4,128)(2,1)S(1)}, bf16[128,1,4,256]{3,2,1,0:T(4,128)(2,1)S(1)}, u32[]{:S(2)}, u32[]{:S(2)}) collective-permute-start(bf16[128,1,4,256]{3,2,1,0:T(4,128)(2,1)S(1)} %get-tuple-element.14), channel_id=1, source_target_pairs={{1,0},{2,1},{3,2},{4,3},{5,4},{6,5},{7,6},{0,7},{9,8},{10,9},{11,1... | collective-permute-start | bytes 786440 | tf_op jit(solution)/shard_map/ppermute | solution.py:18
  33.7 4.4 copy-start
  53.5 10.7 %copy-start.3 = (f32[10,4,256]{2,1,0:T(4,128)S(1)}, f32[10,4,256]{2,1,0:T(4,128)}, u32[]{:S(2)}) copy-start(f32[10,4,256]{2,1,0:T(4,128)} %param.6) | copy-start | bytes 122884
  226.3 18.8 %copy-start.2 = (bf16[128,10,4,256]{3,2,1,0:T(4,128)(2,1)S(1)}, bf16[128,10,4,256]{3,2,1,0:T(4,128)(2,1)}, u32[]{:S(2)}) copy-start(bf16[128,10,4,256]{3,2,1,0:T(4,128)(2,1)} %fusion.7) | copy-start | bytes 7864324
  263.8 1.6 copy-start.4
  263.8 1.6 copy-start.5
  265.3 112.7 %copy-start.8 = (bf16[128,2048]{1,0:T(8,128)(2,1)S(1)}, bf16[128,2048]{1,0:T(8,128)(2,1)}, u32[]{:S(2)}) copy-start(bf16[128,2048]{1,0:T(8,128)(2,1)} %param.7) | copy-start | bytes 1572868
  265.4 112.7 %all-gather.10.cloned.1.call-start = ((), (), s32[]{:S(2)}) async-start(), calls=%async_computation.4 | async-start | bytes 2228224 | tf_op jit(solution)/shard_map/all_gather | solution.py:58
  343.0 83.4 %all-gather.8.cloned.1.call-start = ((), (), s32[]{:S(2)}) async-start(), calls=%async_computation.3 | async-start | bytes 1179648 | tf_op jit(solution)/shard_map/all_gather | solution.py:54
  343.6 119.3 %all-gather.12.cloned.1.call-start = ((), (), s32[]{:S(2)}) async-start(), calls=%async_computation.5 | async-start | bytes 2228224 | tf_op jit(solution)/shard_map/all_gather | solution.py:62
  381.8 136.6 %all-gather.14.cloned.1.call-start = ((), (), s32[]{:S(2)}) async-start(), calls=%async_computation.6 | async-start | bytes 1769472 | tf_op jit(solution)/shard_map/all_gather | solution.py:67
  426.5 40.0 %copy-start.7 = (bf16[2,128,2048]{2,1,0:T(8,128)(2,1)S(1)}, bf16[2,128,2048]{2,1,0:T(8,128)(2,1)}, u32[]{:S(2)}) copy-start(bf16[2,128,2048]{2,1,0:T(8,128)(2,1)} %all-gather.8.cloned.1.call-done) | copy-start | bytes 3145732
  462.9 3.6 copy-start.6
Sparse Core Ops, SparseCore 0:
  10.7 215.5 all-gather.5
  265.5 75.8 reduce-scatter.1
  343.2 34.8 all-gather.9
  380.3 46.1 all-gather.7
  428.1 34.7 all-gather.11
  467.6 50.7 all-gather.13
where the time goes:
time: 532 us; the launch traced here: 531 us
  waiting for transfers between devices  399 us (75%)
  matrix products  50.2 us (9%)
  local copies, waits for them, and re-layouts  36.4 us (7%)
  other arithmetic  26 us (5%)
  between operations  13.7 us (3%)
  starting transfers between devices  6.29 us (1%)
    all_gather x1, waiting for transfers between devices, shards(): piece = lax.all_gather(phi, 'gx', axis=0, tiled=True)  143 us
    reduce_scatter x1, waiting for transfers between devices, shards(): lax.psum_scatter(partial_sums, 'gy', scatter_dimension=2, tiled=True)  75.5 us
    all_gather x1, waiting for transfers between devices, shards(): trio_rows = lax.all_gather(trio, 'gy', axis=2, tiled=True)  50.6 us
    all_gather x1, waiting for transfers between devices, shards(): rows = lax.all_gather(block_pair, 'gy', axis=2, tiled=True)  44.6 us
    all_gather x1, waiting for transfers between devices, shards(): columns = lax.all_gather(pair, 'gx', axis=1, tiled=True)  36.4 us
    all_gather x1, waiting for transfers between devices, shards(): pieces = lax.all_gather(block_pair, 'gx', axis=1, tiled=True)  33.4 us
    slice x4, local copies, waits for them, and re-layouts, shards(): lap = lap + jnp.roll(center, 1, axis) + jnp.roll(center, -1, axis)  30.5 us
    convert_element_type x1, other arithmetic, shards(): hphi = (-0.5 * lap + potential[None] * center).astype(jnp.bfloat16)  19.3 us
  transfers between devices with their start and end apart: 8, of which 8 were waited for; matrix products, arithmetic and copies ran while one was open for 11% of the time, Pallas kernels for 0%

commit v1 on v0

v1 whole, which is shorter than its diff:
```python
import jax
import jax.numpy as jnp
from jax import lax
from jax.experimental import pallas as pl
from jax.experimental.pallas import tpu as pltpu
from jax.sharding import Mesh, PartitionSpec as P

BLOCK = 64
NB = 32
SLOTS = 16
REACH = 8
LANES = 128
ROWS = ("v", "c")
PEERS = ("v", "gy")
BF = jnp.bfloat16
F32 = jnp.float32
I32 = jnp.int32
VMEM_LIMIT = 56 * 1024 * 1024


def iota(shape, dim):
    return lax.broadcasted_iota(I32, shape, dim)


def dot(left, right):
    return lax.dot_general(left, right, (((1,), (0,)), ((), ())), preferred_element_type=F32)


def dot_t(left, right):
    return lax.dot_general(left, right, (((1,), (1,)), ((), ())), preferred_element_type=F32)


def params(**more):
    return pltpu.CompilerParams(vmem_limit_bytes=VMEM_LIMIT, **more)


def pack_kernel(dev, flat, halo, mask_rows, packed, meta):
    rows = flat.shape[0]
    src, dst = iota((512, 512), 0), iota((512, 512), 1)
    wanted = ((dst >> 5) & 3) * 128 + (dst >> 7) * 32 + (dst & 31)
    perm = (src == wanted).astype(F32).astype(BF)
    for x in range(11):
        for half in range(2):
            pieces = []
            for y in range(4):
                at = y * 256 + half * 128
                if x < 10:
                    pieces.append(flat[:, x * 1024 + at : x * 1024 + at + 128])
                else:
                    pieces.append(halo[:, at : at + 128])
            out = dot(jnp.concatenate(pieces, axis=1), perm).astype(BF)
            tile = x if x < 10 else 11
            for j in range(4):
                packed[4 * half + j, :, tile * 128 : tile * 128 + 128] = out[:, j * 128 : j * 128 + 128]
    src, dst = iota((1280, 256), 0), iota((1280, 256), 1)
    plane, lane = src >> 7, src & 127
    low = (dst < 128) & ((lane & 31) == 31) & ((dst & 127) == (lane & 96) + plane)
    high = (dst >= 128) & ((lane & 31) == 0) & ((dst & 127) == (lane & 96) + 16 + plane)
    edges = (low | high).astype(F32).astype(BF)
    found = [dot(packed[v, :, :1280], edges) for v in range(8)]
    for v in range(8):
        tile = found[v][:, :128] + found[(v + 1) % 8][:, 128:]
        packed[v, :, 1280:1408] = tile.astype(BF)
    lane, row = iota((8, LANES), 1), iota((8, LANES), 0)
    total = mask_rows[...]
    start = dev[2] * 10
    for block in range(2):
        for x in range(10):
            part = jnp.abs(flat[block * 64 : block * 64 + 64, x * 1024 : x * 1024 + 1024].astype(F32))
            top = jnp.max(jnp.max(part, axis=0, keepdims=True), axis=1, keepdims=True)
            used = (top > 0.0).astype(F32)
            total = total + jnp.where((row == block) & (lane == start + x), used, 0.0)
    meta[...] = total


def pack(dev, flat, halo, mask_rows):
    vmem = pl.BlockSpec(memory_space=pltpu.VMEM)
    return pl.pallas_call(
        pack_kernel,
        out_shape=(
            jax.ShapeDtypeStruct((8, 128, 1536), BF),
            jax.ShapeDtypeStruct((8, LANES), F32),
        ),
        in_specs=[pl.BlockSpec(memory_space=pltpu.SMEM), vmem, vmem, vmem],
        out_specs=(vmem, vmem),
        compiler_params=params(),
        name="pack",
    )(dev, flat, halo, mask_rows)


def plan_kernel(dev, used_ref, near_ref, table, weights):
    gx, core, gy = dev[0], dev[1], dev[2]
    used = used_ref[...]
    near = near_ref[...]
    square = (LANES, LANES)
    zeros = jnp.zeros((96, LANES), F32)
    tall_used = jnp.concatenate([used, zeros], axis=0)
    tall_near = jnp.concatenate([near, zeros], axis=0)
    a, b = iota(square, 0), iota(square, 1)
    apart = jnp.abs(a - b)
    apart = jnp.minimum(apart, 80 - apart)
    far = ((a < 80) & (b < 80) & (apart > 13)).astype(F32)
    row, lane = iota((NB, LANES), 0), iota((NB, LANES), 1)
    outside = dot(used, far)
    fits = (outside < 0.5) & (lane < 80)
    centre = jnp.min(jnp.where(fits, lane.astype(F32), 127.0), axis=1, keepdims=True)
    key_col = centre * 32.0 + row[:, :1].astype(F32)
    key_row = jnp.sum(jnp.where(row == lane, key_col, 0.0), axis=0, keepdims=True)
    rank_col = jnp.sum(((lane < NB) & (key_row < key_col)).astype(F32), axis=1, keepdims=True)
    rank_row = jnp.sum((key_col < key_row).astype(F32), axis=0, keepdims=True)
    lane_f = lane.astype(F32)
    block_row = jnp.sum(jnp.where(rank_col == lane_f, row.astype(F32), 0.0), axis=0, keepdims=True)
    order = ((rank_row == a.astype(F32)) & (b < NB) & (a < NB)).astype(F32)
    order_rows = order[:NB]
    d8, l8 = iota((8, LANES), 0), iota((8, LANES), 1)
    ahead = l8 - 10 * d8
    ahead = jnp.where(ahead < 0, ahead + 80, ahead)
    touch = ((ahead <= 10) & (l8 < 80)).astype(F32)
    flags = (dot_t(touch, tall_used) > 0.5).astype(F32)
    flags = dot_t(flags, order)
    upper = jnp.where(l8 < SLOTS, pltpu.roll(flags, LANES - SLOTS, 1), 0.0)
    clash = jnp.max(upper * flags)
    sorted_near = dot_t(dot(order_rows, tall_near), order)
    gap = (lane - row) & 31
    stray = (sorted_near > 0.5) & (lane < NB) & (gap > REACH) & (gap < NB - REACH)
    good = (clash < 0.5) & (jnp.max(stray.astype(F32)) < 0.5)
    shift = b - core
    pick = ((a == ((gx + shift) & 15)) & (a < SLOTS)).astype(F32)
    col_half = dot(upper, pick)
    row_half = jnp.sum(jnp.where(l8 == gx, upper, 0.0), axis=1, keepdims=True)
    step = l8 - core
    allowed = ((step >= 0) & (step <= REACH)).astype(F32)
    j, lanes = iota((LANES, 1280), 0), iota((LANES, 1280), 1)
    lanes = jnp.where(lanes >= 640, lanes - 640, lanes)
    widen = ((lanes >> 6) == j).astype(F32)
    for half in range(2):
        mine = gx + 16 * half
        line = jnp.sum(jnp.where(row == mine, sorted_near, 0.0), axis=0, keepdims=True)
        pick = ((a == ((mine + shift) & 31)) & (a < NB)).astype(F32)
        line = dot(jnp.broadcast_to(line, (8, LANES)), pick)
        other = (((mine + step) & 31) >> 4).astype(F32)
        same = (row_half == float(half)) & (col_half == other)
        small = jnp.where(same, line * allowed, 0.0)
        weights[8 * half : 8 * half + 8, :] = dot(small, widen)
    own = jnp.sum(jnp.where(d8 == gy, upper, 0.0), axis=0, keepdims=True)
    source = jnp.where(own > 0.5, pltpu.roll(block_row, LANES - SLOTS, 1), block_row)
    ok = jnp.where(good, 1.0, 0.0)
    out = jnp.where(d8 == 0, source, 0.0) + jnp.where(d8 == 1, block_row, 0.0)
    out = out + jnp.where(d8 == 2, rank_row, 0.0) + jnp.where(d8 == 3, ok, 0.0)
    table[...] = jnp.where(l8 < NB, out, 0.0).astype(I32)


def plan(dev, used, near):
    vmem = pl.BlockSpec(memory_space=pltpu.VMEM)
    return pl.pallas_call(
        plan_kernel,
        out_shape=(
            jax.ShapeDtypeStruct((8, LANES), I32),
            jax.ShapeDtypeStruct((16, 1280), F32),
        ),
        in_specs=[pl.BlockSpec(memory_space=pltpu.SMEM), vmem, vmem],
        out_specs=(vmem, vmem),
        compiler_params=params(),
        name="plan",
    )(dev, used, near)


def sort_columns_kernel(table, mask, kernel, out):
    lane = iota((64, LANES), 1)
    for tile in range(16):
        for rows in range(2):
            halves = []
            for half in range(2):
                block = table[1, 2 * tile + half]
                at = pl.multiple_of((block >> 1) * 128, 128)
                part = kernel[rows * 64 : rows * 64 + 64, pl.ds(at, 128)].astype(F32)
                turned = pltpu.roll(part, 64, 1)
                part = jnp.where((block & 1) == half, part, turned)
                halves.append(part * mask[rows, block].astype(F32))
            both = jnp.where(lane < 64, halves[0], halves[1])
            out[rows * 64 : rows * 64 + 64, tile * 128 : tile * 128 + 128] = both.astype(BF)


def sort_columns(table, mask, kernel):
    vmem = pl.BlockSpec(memory_space=pltpu.VMEM)
    smem = pl.BlockSpec(memory_space=pltpu.SMEM)
    return pl.pallas_call(
        sort_columns_kernel,
        out_shape=jax.ShapeDtypeStruct((128, 2048), BF),
        in_specs=[smem, smem, vmem],
        out_specs=vmem,
        compiler_params=params(),
        name="sort_columns",
    )(table, mask, kernel)


def integrals_kernel(table, dev, own, other, pot, out, right, left_s, left_h):
    slot = pl.program_id(0)
    core = dev[1]
    block = table[0, slot]
    mine = ((block >> 1) & 1) == core
    data = jnp.where(mine, own[0], other[0])
    at = pl.multiple_of(slot * 64, 64)
    lane = iota((64, LANES), 1)
    edge = data[:, 1280:1408].astype(F32)
    swapped = jnp.where((lane & 31) < 16, pltpu.roll(edge, 112, 1), pltpu.roll(edge, 16, 1))
    right[pl.ds(at, 64), :1280] = data[:, :1280]
    right[pl.ds(at, 64), 1280:1408] = swapped.astype(BF)
    right[pl.ds(at, 64), 1408:1536] = data[:, 1408:1536]
    right[pl.ds(at, 64), 1536:1664] = data[:, 1152:1280]

    @pl.when((slot & 1) == core)
    def _():
        to = pl.multiple_of((slot >> 1) * 64, 64)
        left_s[pl.ds(to, 64), :] = data[:, :1280]
        low, high = (lane & 31) == 0, (lane & 31) == 31
        before = jnp.zeros((64, LANES), F32)
        here = data[:, :128].astype(F32)
        for x in range(10):
            after = data[:, x * 128 + 128 : x * 128 + 256].astype(F32) if x < 9 else jnp.zeros((64, LANES), F32)
            near = before + after
            near = near + pltpu.roll(here, 32, 1) + pltpu.roll(here, 96, 1)
            near = near + jnp.where(low, 0.0, pltpu.roll(here, 1, 1))
            near = near + jnp.where(high, 0.0, pltpu.roll(here, 127, 1))
            value = (3.0 + pot[x : x + 1, :]) * here - 0.5 * near
            left_h[pl.ds(to, 64), x * 128 : x * 128 + 128] = value.astype(BF)
            before, here = here, after
        left_h[pl.ds(to, 64), 1280:1408] = (-0.5 * edge).astype(BF)
        left_h[pl.ds(to, 64), 1408:1536] = (-0.5 * data[:, 1152:1280].astype(F32)).astype(BF)
        left_h[pl.ds(to, 64), 1536:1664] = (-0.5 * data[:, 1408:1536].astype(F32)).astype(BF)

    @pl.when(slot == SLOTS - 1)
    def _():
        for chunk in range(4):
            cols = right[chunk * 256 : chunk * 256 + 256, :]
            found = (dot_t(left_s[...], cols[:, :1280]), dot_t(left_h[...], cols))
            for mat in range(2):
                value = found[mat].astype(BF)
                for rows in range(8):
                    for side in range(2):
                        step = (2 * chunk + side - rows) % 8
                        if step < 5:
                            to = mat * 640 + step * 128
                            out[rows * 64 : rows * 64 + 64, to : to + 128] = value[
                                rows * 64 : rows * 64 + 64, side * 128 : side * 128 + 128
                            ]


def integrals(table, dev, own, other, pot):
    def place(parity):
        def index(slot, table, dev):
            block = table[0, slot]
            same = (((block >> 1) & 1) == dev[1]) == (parity == 0)
            return jnp.where(same, (block >> 2) * 2 + (block & 1), 0), 0, 0

        return index

    return pl.pallas_call(
        integrals_kernel,
        grid_spec=pltpu.PrefetchScalarGridSpec(
            num_scalar_prefetch=2,
            grid=(SLOTS,),
            in_specs=[
                pl.BlockSpec((1, 64, 1536), place(0)),
                pl.BlockSpec((1, 64, 1536), place(1)),
                pl.BlockSpec((16, LANES), lambda slot, table, dev: (0, 0)),
            ],
            out_specs=pl.BlockSpec((512, 1280), lambda slot, table, dev: (0, 0)),
            scratch_shapes=[
                pltpu.VMEM((1024, 1664), BF),
                pltpu.VMEM((512, 1280), BF),
                pltpu.VMEM((512, 1664), BF),
            ],
        ),
        out_shape=jax.ShapeDtypeStruct((512, 1280), BF),
        compiler_params=params(dimension_semantics=("arbitrary",)),
        name="integrals",
    )(table, dev, own.reshape(16, 64, 1536), other.reshape(16, 64, 1536), pot)


def combine_kernel(parts, weights, out):
    lines = [jnp.zeros((8, 1280), F32), jnp.zeros((8, 1280), F32)]
    for domain in range(8):
        total = parts[domain].astype(F32)
        for v in range(1, 8):
            total = total + parts[v * 8 + domain].astype(F32)
        for half in range(2):
            lines[half] = lines[half] + total * weights[8 * half + domain : 8 * half + domain + 1, :]
    out[...] = jnp.concatenate(lines, axis=0).astype(BF)


def combine(parts, weights):
    vmem = pl.BlockSpec(memory_space=pltpu.VMEM)
    return pl.pallas_call(
        combine_kernel,
        out_shape=jax.ShapeDtypeStruct((16, 1280), BF),
        in_specs=[vmem, vmem],
        out_specs=vmem,
        compiler_params=params(),
        name="combine",
    )(parts, weights)


def chain_kernel(table, dev, mask, band, k_rows, k_own, out, full, k_all, rows_i, rows_j, first, second, sems):
    gx, gy = dev[0], dev[2]
    copies = []
    for rank in range(NB):
        source = pl.multiple_of(table[1, rank] * 64, 64)
        copy = pltpu.make_async_copy(
            k_rows.at[pl.ds(source, 64), :], k_all.at[rank * 64 : rank * 64 + 64, :], sems.at[rank]
        )
        copy.start()
        copies.append(copy)
    a, b = iota((256, 256), 0), iota((256, 256), 1)
    same_block = (a >> 6) == (b >> 6)
    eye = (a == b).astype(F32).astype(BF)
    empty = jnp.zeros((128, 128), BF)
    for mat in range(2):
        base = mat * 640
        for quad in range(8):
            at = quad * 256
            top = band[at : at + 128, base : base + 640]
            low = band[at + 128 : at + 256, base : base + 640]
            wide = jnp.concatenate(
                [jnp.concatenate([top, empty], axis=1), jnp.concatenate([empty, low], axis=1)], axis=0
            )
            own = wide[:, :256]
            strict = jnp.where(same_block, 0.0, own.astype(F32)).astype(BF)
            own = (own.astype(F32) + dot_t(eye, strict)).astype(BF)
            full[mat, at : at + 256, at : at + 256] = own
            for step in (1, 2):
                to = ((quad + step) % 8) * 256
                part = wide[:, step * 256 : step * 256 + 256]
                full[mat, at : at + 256, to : to + 256] = part
                full[mat, to : to + 256, at : at + 256] = dot_t(eye, part).astype(BF)
            for step in (3, 4, 5):
                to = ((quad + step) % 8) * 256
                full[mat, at : at + 256, to : to + 256] = jnp.zeros((256, 256), BF)
    for mat in range(2):
        for i in range(2):
            rank = pl.multiple_of(table[2, 2 * gx + i] * 64, 64)
            rows_i[mat * 128 + i * 64 : mat * 128 + i * 64 + 64, :] = full[mat, pl.ds(rank, 64), :]
        for j in range(4):
            rank = pl.multiple_of(table[2, 4 * gy + j] * 64, 64)
            rows_j[mat, j * 64 : j * 64 + 64, :] = full[mat, pl.ds(rank, 64), :]
    for copy in copies:
        copy.wait()
    for n in range(8):
        first[:, n * 256 : n * 256 + 256] = dot(rows_i[...], k_all[:, n * 256 : n * 256 + 256]).astype(BF)
    for quad in range(8):
        at = quad * 256
        both = jnp.zeros((256, 256), F32)
        cross = jnp.zeros((128, 256), F32)
        for step in (-2, -1, 0, 1, 2):
            k = ((quad + step) % 8) * 256
            both = both + dot(first[:, k : k + 256], full[0, k : k + 256, at : at + 256])
            cross = cross + dot(first[:128, k : k + 256], full[1, k : k + 256, at : at + 256])
        second[:128, at : at + 256] = (both[128:] + cross).astype(BF)
        second[128:, at : at + 256] = both[:128].astype(BF)
    pair = dot_t(first[128:, :], rows_j[0]) + dot_t(first[:128, :], rows_j[1])
    for n in range(8):
        first[:, n * 256 : n * 256 + 256] = dot(second[...], k_all[:, n * 256 : n * 256 + 256]).astype(BF)
    cubic = dot_t(first[:128, :], rows_j[0]) + dot_t(first[128:, :], rows_j[1])
    grad = 3.0 * pair - 2.0 * cubic
    kernel = k_own[:, pl.ds(pl.multiple_of(gy * 256, 256), 256)].astype(F32)
    r, l = iota((128, 256), 0), iota((128, 256), 1)
    keep = jnp.zeros((128, 256), F32)
    for i in range(2):
        for j in range(4):
            here = ((r >> 6) == i) & ((l >> 6) == j)
            keep = keep + jnp.where(here, mask[i, 4 * gy + j].astype(F32), 0.0)
    out[...] = kernel - 0.5 * (keep * grad)


def chain(table, dev, mask, band, k_rows, k_own):
    vmem = pl.BlockSpec(memory_space=pltpu.VMEM)
    smem = pl.BlockSpec(memory_space=pltpu.SMEM)
    return pl.pallas_call(
        chain_kernel,
        out_shape=jax.ShapeDtypeStruct((128, 256), F32),
        in_specs=[smem, smem, smem, vmem, pl.BlockSpec(memory_space=pl.ANY), vmem],
        out_specs=vmem,
        scratch_shapes=[
            pltpu.VMEM((2, 2048, 2048), BF),
            pltpu.VMEM((2048, 2048), BF),
            pltpu.VMEM((256, 2048), BF),
            pltpu.VMEM((2, 256, 2048), BF),
            pltpu.VMEM((256, 2048), BF),
            pltpu.VMEM((256, 2048), BF),
            pltpu.SemaphoreType.DMA((NB,)),
        ],
        compiler_params=params(),
        name="chain",
    )(table, dev, mask, band, k_rows, k_own)


def extended(block):
    forward = [(i, (i + 1) % 8) for i in range(8)]
    backward = [(target, source) for source, target in forward]
    low = lax.ppermute(block[:, -1:], "gy", forward)
    high = lax.ppermute(block[:, :1], "gy", backward)
    return jnp.concatenate([low, block, high], axis=1)


def spread(values, mask):
    rows, cols = (values.shape[-2], values.shape[-1])
    grid = values.reshape(values.shape[:-2] + (rows // BLOCK, BLOCK, cols // BLOCK, BLOCK))
    return (grid * mask.astype(values.dtype)[:, None, :, None]).reshape(values.shape)


def matmul(left, right):
    return jnp.dot(left, right, preferred_element_type=F32)


def general(phi, potential, kernel, mask_s, mask_k):
    nrows = phi.shape[0]
    width = kernel.shape[1] // 8
    col_start = lax.axis_index("gy") * width
    padded = extended(phi).astype(F32)
    center = padded[:, 1:-1]
    lap = padded[:, 2:] + padded[:, :-2] - 6.0 * center
    for axis in (2, 3):
        lap = lap + jnp.roll(center, 1, axis) + jnp.roll(center, -1, axis)
    hphi = (-0.5 * lap + potential[None] * center).astype(BF)
    flat_phi = phi.reshape(nrows, -1)
    flat_h = hphi.reshape(nrows, -1)
    piece = lax.all_gather(phi, ROWS, axis=0, tiled=True)
    other = piece.reshape(piece.shape[0], -1)
    s_part = jnp.einsum("ap,bp->ab", flat_phi, other, preferred_element_type=F32)
    h_part = jnp.einsum("ap,bp->ab", flat_h, other, preferred_element_type=F32)
    partial_sums = jnp.stack([s_part, h_part])
    mask_cols = lax.dynamic_slice_in_dim(mask_s, col_start // BLOCK, width // BLOCK, 1)
    local = lax.psum_scatter(partial_sums, "gy", scatter_dimension=2, tiled=True)
    block_pair = spread(local, mask_cols).astype(BF)
    rows = lax.all_gather(block_pair, "gy", axis=2, tiled=True)
    k_mat = spread(kernel, mask_k)
    pieces = lax.all_gather(block_pair, ROWS, axis=1, tiled=True)
    x_acc = matmul(k_mat, pieces[0])
    y_acc = matmul(k_mat, pieces[1])
    pair = jnp.stack([x_acc.astype(BF), y_acc.astype(BF)])
    columns = lax.all_gather(pair, ROWS, axis=1, tiled=True)
    p_one = matmul(rows[1], columns[0])
    p_two = matmul(rows[0], columns[1])
    z_mat = matmul(rows[0], columns[0])
    trio = jnp.stack([p_one, z_mat, p_two]).astype(BF)
    trio_rows = lax.all_gather(trio, "gy", axis=2, tiled=True)
    q_mat = (
        matmul(trio_rows[0], columns[0])
        + matmul(trio_rows[1], columns[1])
        + matmul(trio_rows[2], columns[0])
    )
    grad = 3.0 * (trio[0].astype(F32) + trio[2].astype(F32)) - 2.0 * q_mat
    mask_kcols = lax.dynamic_slice_in_dim(mask_k, col_start // BLOCK, width // BLOCK, 1)
    kernel_cols = lax.dynamic_slice_in_dim(kernel, col_start, width, 1).astype(F32)
    return kernel_cols - 0.5 * spread(grad, mask_kcols)


def sparse(phi, potential, kernel, mask_s, mask_k):
    v, core, gy = lax.axis_index("v"), lax.axis_index("c"), lax.axis_index("gy")
    dev = jnp.stack([2 * v + core, core, gy]).astype(I32)
    swap = [(0, 1), (1, 0)]
    halo = lax.ppermute(phi[:, 0].reshape(128, 1024), "gy", [((i + 1) % 8, i) for i in range(8)])
    mask_rows = jnp.pad(mask_s.astype(F32), ((2, 4), (0, LANES - NB)))
    packed, meta = pack(dev, phi.reshape(128, 10240), halo, mask_rows)
    metas = jnp.max(lax.all_gather(meta, "gy"), axis=0)
    metas = lax.all_gather(metas[:4], ROWS)
    used = metas[:, :2].reshape(NB, LANES)
    near = metas[:, 2:].reshape(NB, LANES)
    own = lax.all_to_all(packed, "v", 0, 0, tiled=True)
    other = lax.ppermute(own, "c", swap)
    pot = lax.dynamic_index_in_dim(potential.reshape(10, 4, 8, 32), v, 2, keepdims=False)
    pot = jnp.pad(pot.reshape(10, LANES), ((0, 6), (0, 0)))
    table, weights = plan(dev, used, near)
    k_rows = lax.all_gather(sort_columns(table, mask_k, kernel), ROWS, axis=0, tiled=True)
    part = integrals(table, dev, own, other, pot)
    parts = lax.all_to_all(part.reshape(64, 8, 1280), PEERS, 0, 0, tiled=True)
    mine = combine(parts, weights)
    mine = lax.all_to_all(jnp.broadcast_to(mine[None], (64, 16, 1280)), PEERS, 0, 0, tiled=True)
    theirs = lax.ppermute(mine, "c", swap)
    even = jnp.where(core == 0, mine, theirs)
    odd = jnp.where(core == 0, theirs, mine)
    band = jnp.stack([even, odd]).reshape(2, 8, 8, 2, 8, 1280)
    band = band.transpose(3, 1, 0, 2, 4, 5).reshape(2048, 1280)
    result = chain(table, dev, mask_k, band, k_rows, kernel)
    return result, table[3, 0] == 1


def shards(*args):
    result, fits = sparse(*args)
    return lax.cond(fits, lambda *_: result, general, *args)


def solution(mesh):
    fine = Mesh(mesh.devices.reshape(8, 2, 8), ("v", "c", "gy"))
    in_specs = (
        P(ROWS, "gy", None, None),
        P("gy", None, None),
        P(ROWS, None),
        P(ROWS, None),
        P(ROWS, None),
    )
    out_specs = P(ROWS, "gy")
    return jax.shard_map(shards, mesh=fine, in_specs=in_specs, out_specs=out_specs, check_vma=False)
```

time: 532 us -> 282 us (0.53)
  waiting for transfers between devices: 399 us -> 8.11 us
  blocking collectives: 0 us -> 184 us
  matrix products: 50.2 us -> 0 us
  Pallas kernels: 0 us -> 45.3 us
  other arithmetic: 26 us -> 3.22 us
  local copies, waits for them, and re-layouts: 36.4 us -> 14.6 us
    all_gather x5 -> x1, waiting for transfers between devices: 308 us -> 0.01 us  [sparse(): lax.all_gather(sort_columns(table, mask_k, kernel), ROWS, axis=0, tiled=T...]
    all_to_all x0 -> x3, blocking collectives: none -> 129 us  [the longest x1 61.6 us: sparse(): own = lax.all_to_all(packed, 'v', 0, 0, tiled=True)]
    reduce_scatter x1 -> x0, waiting for transfers between devices: 75.5 us -> none  [shards(): lax.psum_scatter(partial_sums, 'gy', scatter_dimension=2, tiled=True)]
    all_gather x0 -> x2, blocking collectives: none -> 55.2 us  [the longest x1 27.9 us: sparse(): metas = jnp.max(lax.all_gather(meta, 'gy'), axis=0)]
    dot_general x10 -> x0, matrix products: 50.2 us -> none  [the longest x1 18.8 us: shards(): jnp.einsum('ap,bp->ab', flat_phi, other, preferred_element_type=jnp.float32)]
    pallas_call x0 -> x6, Pallas kernels: none -> 45.3 us  [the longest x1 16.7 us: integrals(): pl.pallas_call(integrals_kernel, grid_spec=pltpu.PrefetchScalarGridSpec(n...]
    slice x5 -> x3, local copies, waits for them, and re-layouts: 30.7 us -> 2.87 us  [the longest x1 1.19 us: sparse(): return (result, table[3, 0] == 1)]
    convert_element_type x5 -> x1, other arithmetic: 23.1 us -> 0.01 us  [sparse(): mask_rows = jnp.pad(mask_s.astype(F32), ((2, 4), (0, LANES - NB)))]
  transfers between devices with their start and end apart: 8 -> 4, of which waited for: 8 -> 2; matrix products, arithmetic and copies ran while one was open for 11% -> 5% of each run, Pallas kernels for 0% -> 7%
where the time goes in v1:
time: 282 us; the launch traced here: 281 us
  blocking collectives  184 us (65%)
  Pallas kernels  45.3 us (16%)
  local copies, waits for them, and re-layouts  14.6 us (5%)
  between operations  14.2 us (5%)
  starting transfers between devices  11.5 us (4%)
  waiting for transfers between devices  8.11 us (3%)
  other arithmetic  3.22 us (1%)
    all_to_all x1, blocking collectives, sparse(): own = lax.all_to_all(packed, 'v', 0, 0, tiled=True)  61.6 us
    all_to_all x1, blocking collectives, sparse(): lax.all_to_all(jnp.broadcast_to(mine[None], (64, 16, 1280)), PEERS, 0, 0,...  38.2 us
    all_to_all x1, blocking collectives, sparse(): parts = lax.all_to_all(part.reshape(64, 8, 1280), PEERS, 0, 0, tiled=True)  29.5 us
    all_gather x1, blocking collectives, sparse(): metas = jnp.max(lax.all_gather(meta, 'gy'), axis=0)  27.9 us
    all_gather x1, blocking collectives, sparse(): metas = lax.all_gather(metas[:4], ROWS)  27.2 us
    pallas_call x1, Pallas kernels, integrals(): pl.pallas_call(integrals_kernel, grid_spec=pltpu.PrefetchScalarGridSpec(n...  16.7 us
    pallas_call x1, Pallas kernels, chain(): pl.pallas_call(chain_kernel, out_shape=jax.ShapeDtypeStruct((128, 256), F...  16 us
    pallas_call x1, Pallas kernels, pack(): pl.pallas_call(pack_kernel, out_shape=(jax.ShapeDtypeStruct((8, 128, 1536...  6.04 us
  transfers between devices with their start and end apart: 4, of which 2 were waited for; matrix products, arithmetic and copies ran while one was open for 5% of the time, Pallas kernels for 7%

profile of v1, /device:TPU:1, one launch (start us, length us, event | category | flops | bytes accessed | tf_op | source)
XLA Modules:
  0.0 281.5 jit_solution(15480967130968173932)
XLA Ops:
  6.5 0.0 copy-start.13
  6.5 0.0 all-gather.20.cloned.1.call-start
  6.5 1.1 slice.104
  7.6 6.0 %collective-permute-start.2 = (bf16[128,1024]{1,0:T(8,128)(2,1)S(1)}, bf16[128,1024]{1,0:T(8,128)(2,1)S(1)}, u32[]{:S(2)}, u32[]{:S(2)}) collective-permute-start(bf16[128,1024]{1,0:T(8,128)(2,1)S(1)} %bitcast.90), channel_id=1, source_target_pairs={{1,0},{2,1},{3,2},{4,3},{5,4},{6,5},{7,6},{0,7},{9,8},{10,9},{11,1... | collective-permute-start | bytes 786440 | tf_op jit(solution)/shard_map/ppermute | solution.py:462
  13.6 0.0 copy-start.7
  13.6 4.9 %reshape.59.flat = bf16[128,10240]{1,0:T(8,128)(2,1)} reshape(bf16[128,10,4,256]{3,2,1,0:T(4,128)(2,1)} %param.7) | data formatting | bytes 5242880 | tf_op jit(solution)/shard_map/reshape | solution.py:464
  18.6 0.0 copy-done.13
  18.6 0.6 pad.8.mask_rows
  19.2 0.7 pad_add_fusion.dev
  19.8 0.0 collective-permute-done.2.halo
  19.8 0.0 copy-start.9
  19.8 0.7 copy-done.9
  20.5 6.0 %pack.1 = (bf16[8,128,1536]{2,1,0:T(8,128)(2,1)}, f32[8,128]{1,0:T(8,128)}) custom-call(s32[3]{0:T(128)} %pad_add_fusion.dev, bf16[128,10240]{1,0:T(8,128)(2,1)} %reshape.59.flat, bf16[128,1024]{1,0:T(8,128)(2,1)} %copy-done.9, f32[8,128]{1,0:T(8,128)} %pad.8.mask_rows), custom_call_target="tpu_custom_call" | custom-call | tf_op jit(solution)/shard_map/pack/pallas_call | solution.py:78
  26.6 27.9 %all-gather = f32[64,128]{1,0:T(8,128)S(1)} all-gather(f32[8,128]{1,0:T(8,128)} %get-tuple-element.28), channel_id=2, replica_groups=mesh['v'=8,'c'=2,'gy'=8] {'gy'}, dimensions={0}, use_global_device_ids=true | all-gather | bytes 36864 | tf_op jit(solution)/shard_map/all_gather | solution.py:465
  54.5 27.2 %all-gather.2 = f32[16,4,128]{2,1,0:T(4,128)S(1)} all-gather(f32[1,4,128]{2,1,0:T(4,128)S(1)} %slice_bitcast_fusion.23), channel_id=3, replica_groups=mesh['v'=8,'c'=2,'gy'=8] {'v','c'}, dimensions={0}, use_global_device_ids=true | all-gather | bytes 34816 | tf_op jit(solution)/shard_map/all_gather | solution.py:466
  81.7 0.6 fusion.38
  82.4 2.3 plan.1
  84.6 0.0 copy-done.7
  84.6 0.0 copy-done.12
  84.6 2.1 sort_columns.1
  86.7 0.0 all-gather.20.cloned.1.call-update
  86.8 0.0 copy-start.10
  86.8 61.6 %all_to_all.15 = bf16[8,128,1536]{2,1,0:T(8,128)(2,1)S(1)} all-to-all(bf16[8,128,1536]{2,1,0:T(8,128)(2,1)} %get-tuple-element.30), channel_id=1, replica_groups=mesh['v'=8,'c'=2,'gy'=8] {'v'}, dimensions={0} | all-to-all | bytes 6291456 | tf_op jit(solution)/shard_map/all_to_all | solution.py:469
  148.4 0.0 copy-start.5
  148.4 2.4 collective-permute-start.3
  150.8 0.0 copy-done.10
  150.8 0.1 reshape.64
  151.0 0.1 reshape.65
  151.0 0.6 pad.9.pot
  151.7 5.3 %collective-permute-done.3 = bf16[8,128,1536]{2,1,0:T(8,128)(2,1)} collective-permute-done((bf16[8,128,1536]{2,1,0:T(8,128)(2,1)S(1)}, bf16[8,128,1536]{2,1,0:T(8,128)(2,1)}, u32[]{:S(2)}, u32[]{:S(2)}) %collective-permute-start.3) | collective-permute-done | bytes 3145760 | tf_op jit(solution)/shard_map/ppermute | solution.py:470
  156.9 0.0 copy-done.5
  156.9 16.7 %integrals.1 = bf16[512,1280]{1,0:T(8,128)(2,1)} custom-call(s32[8,128]{1,0:T(8,128)} %get-tuple-element.29.table, s32[3]{0:T(128)} %pad_add_fusion.dev, bf16[16,64,1536]{2,1,0:T(8,128)(2,1)} %bitcast.85, bf16[16,64,1536]{2,1,0:T(8,128)(2,1)} %bitcast.30.other, f32[16,128]{1,0:T(8,128)} %pad.9.pot), custom_call_target="tpu_custom_call" | custom-call | tf_op jit(solution)/shard_map/integrals/pallas_call | solution.py:258
  173.7 29.5 %all_to_all.16.parts = bf16[64,8,1280]{2,1,0:T(8,128)(2,1)} all-to-all(bf16[64,8,1280]{2,1,0:T(8,128)(2,1)} %bitcast.88), channel_id=1, replica_groups=mesh['v'=8,'c'=2,'gy'=8] {'v','gy'}, dimensions={0} | all-to-all | bytes 2621440 | tf_op jit(solution)/shard_map/all_to_all | solution.py:476
  203.1 2.2 combine.1
  205.3 0.9 broadcast_in_dim.2
  206.2 38.2 %all_to_all.17 = bf16[64,16,1280]{2,1,0:T(8,128)(2,1)S(1)} all-to-all(bf16[64,16,1280]{2,1,0:T(8,128)(2,1)S(1)} %broadcast_in_dim.2), channel_id=1, replica_groups=mesh['v'=8,'c'=2,'gy'=8] {'v','gy'}, dimensions={0} | all-to-all | bytes 5242880 | tf_op jit(solution)/shard_map/all_to_all | solution.py:478
  244.5 3.1 %collective-permute-start.4 = (bf16[64,16,1280]{2,1,0:T(8,128)(2,1)S(1)}, bf16[64,16,1280]{2,1,0:T(8,128)(2,1)}, u32[]{:S(2)}, u32[]{:S(2)}) collective-permute-start(bf16[64,16,1280]{2,1,0:T(8,128)(2,1)S(1)} %all_to_all.17), channel_id=1, source_target_pairs={{0,8},{8,0},{1,9},{9,1},{2,10},{10,2},{3,11},{11,3},{4,12},{12,4},... | collective-permute-start | bytes 7864328 | tf_op jit(solution)/shard_map/ppermute | solution.py:479
  247.6 1.2 slice.108
  249.4 2.8 %collective-permute-done.4 = bf16[64,16,1280]{2,1,0:T(8,128)(2,1)} collective-permute-done((bf16[64,16,1280]{2,1,0:T(8,128)(2,1)S(1)}, bf16[64,16,1280]{2,1,0:T(8,128)(2,1)}, u32[]{:S(2)}, u32[]{:S(2)}) %collective-permute-start.4) | collective-permute-done | bytes 2621472 | tf_op jit(solution)/shard_map/ppermute | solution.py:479
  252.3 2.1 broadcast_select_fusion.1
  254.3 0.5 maximum_bitcast_fusion
  254.8 0.0 copy-start.8
  254.8 3.1 %copy.14 = bf16[2,8,2,8,8,1280]{5,4,3,2,1,0:T(8,128)(2,1)} copy(bf16[2,8,2,8,8,1280]{5,4,0,3,1,2:T(8,128)(2,1)S(1)} %maximum_bitcast_fusion) | data formatting | bytes 10485760 | tf_op jit(solution)/shard_map/transpose | solution.py:483
  257.9 0.0 copy-done.8
  257.9 16.0 %chain.1 = f32[128,256]{1,0:T(8,128)S(1)} custom-call(s32[8,128]{1,0:T(8,128)} %get-tuple-element.29.table, s32[3]{0:T(128)} %pad_add_fusion.dev, s32[2,32]{1,0:T(2,128)S(1)} %copy-done.12, bf16[2048,1280]{1,0:T(8,128)(2,1)} %bitcast.84, bf16[2048,2048]{1,0:T(8,128)(2,1)} %all-gather.20.cloned.1.call-done.k_rows, bf16[128,2048]{1,0:T(8,128)(2,1)S(1)} %copy-done.8), custom_call_target="tpu_custom_call" | custom-call | tf_op jit(solution)/shard_map/chain/pallas_call | solution.py:378
  274.0 0.0 copy-done.2
  274.0 0.0 copy-start.11
  274.0 0.6 copy-done.11
  (9 shorter events, 0.1 us)
Async XLA Ops:
  6.5 12.0 %copy-start.13 = (s32[2,32]{1,0:T(2,128)S(1)}, s32[2,32]{1,0:T(2,128)}, u32[]{:S(2)}) copy-start(s32[2,32]{1,0:T(2,128)} %param.10) | copy-start | bytes 772
  6.5 251.4 %all-gather.20.cloned.1.call-start = ((), (), s32[]{:S(2)}) async-start(), calls=%async_computation.10 | async-start | bytes 8912896 | tf_op jit(solution)/shard_map/all_gather | solution.py:474
  7.6 12.2 %collective-permute-start.2 = (bf16[128,1024]{1,0:T(8,128)(2,1)S(1)}, bf16[128,1024]{1,0:T(8,128)(2,1)S(1)}, u32[]{:S(2)}, u32[]{:S(2)}) collective-permute-start(bf16[128,1024]{1,0:T(8,128)(2,1)S(1)} %bitcast.90), channel_id=1, source_target_pairs={{1,0},{2,1},{3,2},{4,3},{5,4},{6,5},{7,6},{0,7},{9,8},{10,9},{11,1... | collective-permute-start | bytes 786440 | tf_op jit(solution)/shard_map/ppermute | solution.py:462
  13.6 71.0 %copy-start.7 = (bf16[128,2048]{1,0:T(8,128)(2,1)S(1)}, bf16[128,2048]{1,0:T(8,128)(2,1)}, u32[]{:S(2)}) copy-start(bf16[128,2048]{1,0:T(8,128)(2,1)} %k_own.1) | copy-start | bytes 1572868
  13.6 71.0 %copy-start.12 = (s32[2,32]{1,0:T(2,128)S(1)}, s32[2,32]{1,0:T(2,128)}, u32[]{:S(2)}) copy-start(s32[2,32]{1,0:T(2,128)} %mask.3) | copy-start | bytes 772
  19.8 0.7 copy-start.9
  86.8 64.1 %copy-start.10 = (f32[10,4,256]{2,1,0:T(4,128)S(1)}, f32[10,4,256]{2,1,0:T(4,128)}, u32[]{:S(2)}) copy-start(f32[10,4,256]{2,1,0:T(4,128)} %param.8) | copy-start | bytes 122884
  148.4 8.5 %copy-start.5 = (bf16[8,128,1536]{2,1,0:T(8,128)(2,1)}, bf16[8,128,1536]{2,1,0:T(8,128)(2,1)S(1)}, u32[]{:S(2)}) copy-start(bf16[8,128,1536]{2,1,0:T(8,128)(2,1)S(1)} %all_to_all.15) | copy-start | bytes 9437188
  148.4 8.5 %collective-permute-start.3 = (bf16[8,128,1536]{2,1,0:T(8,128)(2,1)S(1)}, bf16[8,128,1536]{2,1,0:T(8,128)(2,1)}, u32[]{:S(2)}, u32[]{:S(2)}) collective-permute-start(bf16[8,128,1536]{2,1,0:T(8,128)(2,1)S(1)} %all_to_all.15), channel_id=1, source_target_pairs={{0,8},{8,0},{1,9},{9,1},{2,10},{10,2},{3,11},{11,3},{4,12},{12,4},... | collective-permute-start | bytes 9437192 | tf_op jit(solution)/shard_map/ppermute | solution.py:470
  244.5 7.8 %collective-permute-start.4 = (bf16[64,16,1280]{2,1,0:T(8,128)(2,1)S(1)}, bf16[64,16,1280]{2,1,0:T(8,128)(2,1)}, u32[]{:S(2)}, u32[]{:S(2)}) collective-permute-start(bf16[64,16,1280]{2,1,0:T(8,128)(2,1)S(1)} %all_to_all.17), channel_id=1, source_target_pairs={{0,8},{8,0},{1,9},{9,1},{2,10},{10,2},{3,11},{11,3},{4,12},{12,4},... | collective-permute-start | bytes 7864328 | tf_op jit(solution)/shard_map/ppermute | solution.py:479
  254.8 3.1 %copy-start.8 = (bf16[128,2048]{1,0:T(8,128)(2,1)S(1)}, bf16[128,2048]{1,0:T(8,128)(2,1)}, u32[]{:S(2)}) copy-start(bf16[128,2048]{1,0:T(8,128)(2,1)} %k_own.1) | copy-start | bytes 1572868
  257.9 16.0 %copy-start.2 = (bf16[128,10,4,256]{3,2,1,0:T(4,128)(2,1)S(1)}, bf16[128,10,4,256]{3,2,1,0:T(4,128)(2,1)}, u32[]{:S(2)}) copy-start(bf16[128,10,4,256]{3,2,1,0:T(4,128)(2,1)} %param.7) | copy-start | bytes 7864324
  274.0 0.7 copy-start.11
Sparse Core Ops, SparseCore 0:
  86.9 81.2 all-gather.19
